TPU v7x, 32 devices: a whole 2x2x4 slice. The times are simulated.
32 devices in a mesh: grp: 1, row: 8 (over z, y), col: 4 (over x, core).
Axes of the slice: x: 2, y: 2, z: 4, core: 2. Of those that a mesh axis runs over, the one named last changes fastest.
Arguments:
- pair_act: bfloat16 [128, 128, 128], P(('grp', 'row'), 'col'), may hold values from -6 to 6
- single: bfloat16 [128, 768], P(('grp', 'row')), may hold values from -6 to 6
- token_mask: int32 [128], P('grp'), may hold values from 0 to 1, as said below
- chain_index: int32 [128], P('grp'), may hold values from 0 to 7, never falling along the last dimension, each value on 1 to 32 neighbouring positions
- residue_index: int32 [128], P('grp'), may hold values from 1 to 192, as said below
- tri_gain: float32 [2, 128], replicated, may hold values from 0.25 to 1.75
- tri_qk: bfloat16 [2, 128, 256], replicated, may hold values from -1.5 to 1.5
- tri_vg: bfloat16 [2, 128, 256], replicated, may hold values from -0.5 to 0.5
- tri_out: bfloat16 [2, 128, 128], replicated, may hold values from -0.5 to 0.5
- bias_gain: float32 [128], replicated, may hold values from 0.25 to 1.75
- bias_proj: bfloat16 [128, 16], replicated, may hold values from -0.5 to 0.5
- chain_bias: float32 [16], P('col'), may hold values from -4 to 4
- pos_slope: float32 [16], P('col'), may hold values from -6 to 6
- attn_gain: float32 [768], replicated, may hold values from 0.25 to 1.75
- attn_qk: bfloat16 [2, 768, 768], P(None, None, 'col'), may hold values from -0.375 to 0.375
- attn_vg: bfloat16 [2, 768, 768], P(None, None, 'col'), may hold values from -0.21875 to 0.21875
- attn_out: bfloat16 [768, 768], P('col'), may hold values from -0.875 to 0.875
Outputs:
- pair_out: bfloat16 [128, 128, 128], P(('grp', 'row'), 'col')
- token_update: bfloat16 [128, 768], P(('grp', 'row'), 'col')
Inputs may be any that keep to these rules, and one draw needn't show every extreme that they name: `token_mask`: 1 on a leading run of at least 64 positions, 0 on the rest, and some position is 0. `chain_index`: never decreasing along the positions; all 8 chains occur. `residue_index`: starts at 1 and rises by 1 or 2 from each position to the next, by 2 at exactly 64 of them.
All inputs are finite; a program needn't handle non-finite values.
Results may differ from a plain program's by a relative error of at most 0.019.
Values may be sent and summed in bfloat16 or wider, within the bound.
A program may use at most 64 MiB of HBM per device.

v0:
```python
import functools
import math

import jax
import jax.numpy as jnp
from jax import lax
from jax.experimental import pallas as pl
from jax.experimental.pallas import tpu as pltpu
from jax.sharding import PartitionSpec as P

C = 128
TRI_HEADS = 8
TRI_DIM = 16
HEAD_DIM = 48

epsilon = 1e-05
cap_value = 10.0
rel_reach = 32.0
MESH = pl.DeviceIdType.MESH
f32 = jnp.float32
bf16 = jnp.bfloat16


def layer_norm(inputs, norm_gain):
    inputs = inputs.astype(f32)
    centered = inputs - jnp.mean(inputs, -1, keepdims=True)
    spread = jnp.mean(centered * centered, -1, keepdims=True)
    return centered * lax.rsqrt(spread + epsilon) * norm_gain


def feature(inputs):
    return jnp.where(inputs > 0, inputs + 1.0, jnp.exp(jnp.minimum(inputs, 0.0)))


def sigmoid(inputs):
    return 1.0 / (1.0 + jnp.exp(-inputs))


def dot(left, right):
    return jnp.dot(left, right, preferred_element_type=f32)


def dot_nt(left, right):
    return lax.dot_general(left, right, (((1,), (1,)), ((), ())), preferred_element_type=f32)


def dot_tn(left, right):
    return lax.dot_general(left, right, (((0,), (0,)), ((), ())), preferred_element_type=f32)


def iota(shape, dim):
    return lax.broadcasted_iota(jnp.int32, shape, dim)


def log2(number):
    power = number.bit_length() - 1
    assert 1 << power == number
    return power


def kernel(
    n_row,
    n_col,
    pair_ref,
    single_ref,
    mask_ref,
    chain_ref,
    residue_ref,
    gain_ref,
    qk_ref,
    vg_ref,
    out_ref,
    bias_gain_ref,
    bias_proj_ref,
    chain_bias_ref,
    slope_ref,
    attn_gain_ref,
    aqk_hbm,
    avg_hbm,
    aout_hbm,
    pair_out_ref,
    token_ref,
    aqk_ref,
    avg_ref,
    aout_ref,
    row_part,
    row_recv,
    col_part,
    col_recv,
    col_full,
    q_wide,
    kv,
    kv_own,
    query_gates,
    rel,
    aout_send,
    aout_full,
    num_send,
    num_recv,
    den_send,
    den_recv,
    load_sem,
    row_send_sem,
    row_recv_sem,
    rs_send_sem,
    rs_recv_sem,
    ag_send_sem,
    ag_recv_sem,
    kv_send_sem,
    kv_recv_sem,
    own_send_sem,
    own_recv_sem,
    qg_send_sem,
    qg_recv_sem,
    rel_send_sem,
    rel_recv_sem,
    aout_send_sem,
    aout_recv_sem,
    num_send_sem,
    num_recv_sem,
    den_send_sem,
    den_recv_sem,
):
    my_row = lax.axis_index("row")
    my_col = lax.axis_index("col")
    rows, cols, _ = pair_ref.shape
    tokens = mask_ref.shape[1]
    flat = rows * cols
    row_first = my_row * rows
    col_first = my_col * cols
    heads_here = chain_bias_ref.shape[1]
    heads = heads_here * n_col
    width = token_ref.shape[1]
    per = cols // rows
    tri_scale = 1.0 / (2.0 * TRI_DIM * math.sqrt(tokens))
    col_peers = [lax.rem(my_col + d, n_col) for d in range(n_col)]
    row_peers = [lax.rem(my_row + d, n_row) for d in range(n_row)]
    far_first = sorted(range(1, n_row), key=lambda d: abs(2 * d - n_row))
    pushed = []

    def push(src, dst, send_sem, recv_sem, where):
        copy = pltpu.make_async_remote_copy(
            src_ref=src, dst_ref=dst, send_sem=send_sem, recv_sem=recv_sem,
            device_id=where, device_id_type=MESH,
        )
        copy.start()
        pushed.append(copy)
        return copy

    def push_cols(src_of, dst_of, send_sem, recv_sem):
        return [
            push(src_of(d), dst_of(d), send_sem.at[d - 1], recv_sem.at[d - 1], {"col": col_peers[d]})
            for d in range(1, n_col)
        ]

    barrier = pltpu.get_barrier_semaphore()
    for d in range(1, n_col):
        pl.semaphore_signal(barrier, inc=1, device_id={"col": col_peers[d]}, device_id_type=MESH)
    for d in range(1, n_row):
        pl.semaphore_signal(barrier, inc=1, device_id={"row": row_peers[d]}, device_id_type=MESH)
    loads = []
    for position, (src, dst) in enumerate(((aqk_hbm, aqk_ref), (avg_hbm, avg_ref), (aout_hbm, aout_ref))):
        loads.append(pltpu.make_async_copy(src, dst, load_sem.at[position]))
        loads[-1].start()

    length = jnp.sum(mask_ref[...].astype(f32), axis=1, keepdims=True)

    pair = pair_ref[...].reshape(flat, C)
    normed = layer_norm(pair, gain_ref[0:1, :]).astype(bf16)
    key_value = dot(normed, jnp.concatenate([qk_ref[0, :, C:], vg_ref[0, :, :C]], axis=1))
    col_pos = (iota((1, cols, C), 1) + col_first).astype(f32)
    col_keep = col_pos < length.reshape(1, 1, 1)
    key_feat = jnp.where(col_keep, feature(key_value[:, :C]).reshape(rows, cols, C), 0.0).astype(bf16)
    values = key_value[:, C:].astype(bf16).reshape(rows, cols, C)
    dim_shift = log2(TRI_DIM)
    left = iota((C, C), 0)
    right = iota((C, C), 1)
    same_head = (left >> dim_shift) == (right >> dim_shift)
    for i in range(rows):
        outer = jnp.where(same_head, dot_tn(key_feat[i], values[i]), 0.0)
        row_part[i] = jnp.sum(outer.reshape(TRI_HEADS, TRI_DIM, C), axis=0).astype(bf16)
    pl.semaphore_wait(barrier, n_row + n_col - 2)
    row_copies = push_cols(lambda d: row_part, lambda d: row_recv.at[d - 1], row_send_sem, row_recv_sem)

    lane = iota((8, C), 1)
    top = iota((8, C), 0) == 0
    relation = jnp.zeros((8, C), f32)
    for h in range(heads_here):
        pick = jnp.where(top, chain_bias_ref[:, h:h + 1], slope_ref[:, h:h + 1])
        relation = relation + jnp.where(lane == my_col * heads_here + h, pick, 0.0)
    rel[my_col] = relation
    rel_copies = push_cols(lambda d: rel.at[my_col], lambda d: rel.at[my_col], rel_send_sem, rel_recv_sem)
    tok = layer_norm(single_ref[...], attn_gain_ref[...]).astype(bf16)
    loads[0].wait()
    loads[1].wait()
    kv[my_row, 0] = dot_nt(tok, aqk_ref[1]).astype(bf16)
    kv[my_row, 1] = dot_nt(tok, avg_ref[0]).astype(bf16)
    kv_copies = {}
    for d in far_first:
        kv_copies[d] = push(kv.at[my_row], kv.at[my_row], kv_send_sem.at[d - 1],
                            kv_recv_sem.at[d - 1], {"row": row_peers[d]})
    query_gate = dot(normed, jnp.concatenate([qk_ref[0, :, :C], vg_ref[0, :, C:]], axis=1))
    query_feat = feature(query_gate[:, :C]).astype(bf16).reshape(rows, cols, C)
    gate = sigmoid(query_gate[:, C:]) * tri_scale
    query_gates[my_col, 0] = dot_nt(tok, aqk_ref[0]).astype(bf16)
    query_gates[my_col, 1] = sigmoid(dot_nt(tok, avg_ref[1])).astype(bf16)
    loads[2].wait()
    for c in range(n_col):
        aout_send[c] = aout_ref[:, c * width:(c + 1) * width]
    aout_full[my_col] = aout_send[my_col]

    for copy in row_copies:
        copy.wait_recv()
    qg_copies = push_cols(lambda d: query_gates.at[my_col], lambda d: query_gates.at[my_col],
                          qg_send_sem, qg_recv_sem)
    states = row_part[...].astype(f32)
    for d in range(1, n_col):
        states = states + row_recv[d - 1].astype(f32)
    states = states.astype(bf16)
    mixed = []
    for i in range(rows):
        block = jnp.concatenate([states[i]] * TRI_HEADS, axis=0)
        block = jnp.where(same_head, block, jnp.zeros_like(block))
        mixed.append(dot(query_feat[i], block))
    mixed = jnp.concatenate(mixed, axis=0)
    update = (gate * mixed).astype(bf16)
    pair = (pair.astype(f32) + dot(update, out_ref[0])).astype(bf16)

    normed = layer_norm(pair, gain_ref[1:2, :]).astype(bf16)
    key_value = dot(normed, jnp.concatenate([qk_ref[1, :, C:], vg_ref[1, :, :C]], axis=1))
    row_pos = (iota((rows, 1, C), 0) + row_first).astype(f32)
    row_keep = row_pos < length.reshape(1, 1, 1)
    key_feat = jnp.where(row_keep, feature(key_value[:, :C]).reshape(rows, cols, C), 0.0)
    key_feat = key_feat.astype(bf16).reshape(flat, C)
    values = key_value[:, C:]
    entry = jnp.where(same_head, left & (TRI_DIM - 1), -1)
    share = TRI_DIM // n_row

    def spread(first, count):
        parts = [(entry == first + s).astype(f32).astype(bf16) for s in range(count)]
        return parts[0] if count == 1 else jnp.concatenate(parts, axis=1)

    rs_copies = {}
    for d in far_first + [0]:
        owner = row_peers[d]
        wide = dot(key_feat, spread(owner * share, share))
        for s in range(share):
            part = wide[:, s * C:(s + 1) * C] * values
            col_part[owner, s] = jnp.sum(part.reshape(rows, cols, C), axis=0).astype(bf16)
        if d:
            rs_copies[d] = push(col_part.at[owner], col_recv.at[d - 1], rs_send_sem.at[d - 1],
                                rs_recv_sem.at[d - 1], {"row": owner})
    aout_copies = push_cols(lambda d: aout_send.at[col_peers[d]], lambda d: aout_full.at[my_col],
                            aout_send_sem, aout_recv_sem)
    query_gate = dot(normed, jnp.concatenate([qk_ref[1, :, :C], vg_ref[1, :, C:]], axis=1))
    query_feat = feature(query_gate[:, :C]).astype(bf16)
    gate = sigmoid(query_gate[:, C:]) * tri_scale
    for e in range(0, TRI_DIM, 2):
        wide = dot(query_feat, spread(e, 2)).astype(bf16)
        q_wide[e] = wide[:, :C]
        q_wide[e + 1] = wide[:, C:]
    for d in far_first:
        kv_copies[d].wait_recv()
    kv_own[my_col] = kv[pl.ds(my_col * per, per)]
    own_copies = push_cols(lambda d: kv.at[pl.ds(col_peers[d] * per, per)], lambda d: kv_own.at[my_col],
                           own_send_sem, own_recv_sem)
    total = col_part[my_row].astype(f32)
    for d in far_first:
        rs_copies[d].wait_recv()
        total = total + col_recv[d - 1].astype(f32)
    col_full[my_row] = total.astype(bf16)
    ag_copies = {}
    for d in far_first:
        ag_copies[d] = push(col_full.at[my_row], col_full.at[my_row], ag_send_sem.at[d - 1],
                            ag_recv_sem.at[d - 1], {"row": row_peers[d]})

    head_shift = log2(heads)
    lines = rows * heads
    for copy in rel_copies + qg_copies + own_copies:
        copy.wait_recv()
    head_of = iota((heads, width), 0)
    head_lane = iota((heads, width), 1)
    lanes_of = []
    for c in range(n_col):
        start = (head_of - c * heads_here) * HEAD_DIM
        lanes_of.append((head_lane >= start) & (head_lane < start + HEAD_DIM))
    scores = jnp.zeros((lines, cols), f32)
    for c in range(n_col):
        query = query_gates[c, 0].astype(f32)
        stack = jnp.where(lanes_of[c][None], query[:, None, :], 0.0).reshape(lines, width).astype(bf16)
        scores = scores + dot_nt(stack, kv_own[c, :, 0].reshape(cols, width))
    scores = scores * (1.0 / math.sqrt(HEAD_DIM))
    here = iota((lines, tokens), 1) == (iota((lines, tokens), 0) >> head_shift) + row_first
    chain = chain_ref[...].astype(f32)
    residue = residue_ref[...]
    my_chain = jnp.sum(jnp.where(here, chain, 0.0), axis=1, keepdims=True)
    my_residue = jnp.sum(jnp.where(here, residue.astype(f32), 0.0), axis=1, keepdims=True)
    relation = rel[0]
    for c in range(1, n_col):
        relation = relation + rel[c]
    own_head = iota((lines, C), 1) == (iota((lines, C), 0) & (heads - 1))
    my_bias = jnp.sum(jnp.where(own_head, relation[0:1], 0.0), axis=1, keepdims=True)
    my_slope = jnp.sum(jnp.where(own_head, relation[1:2], 0.0), axis=1, keepdims=True)
    kind = iota((8, tokens), 0)
    facts = jnp.where(kind == 0, chain, jnp.where(kind == 1, (residue >> 4).astype(f32),
                                                  (residue & 15).astype(f32))).astype(bf16)
    take = (iota((tokens, cols), 0) == iota((tokens, cols), 1) + col_first).astype(f32).astype(bf16)
    facts = dot(facts, take)
    offset = my_residue - (facts[1:2] * 16.0 + facts[2:3])
    offset = jnp.clip(offset, -rel_reach, rel_reach) * (1.0 / rel_reach)
    scores = scores + jnp.where(my_chain == facts[0:1], my_bias + my_slope * offset, 0.0)
    real = (iota((lines, cols), 1) + col_first).astype(f32) < length

    def mix(chunk):
        part = None
        for s in range(share):
            term = (q_wide[chunk * share + s].astype(f32).reshape(rows, cols, C)
                    * col_full[chunk, s].astype(f32).reshape(1, cols, C))
            part = term if part is None else part + term
        return part

    mixed = mix(my_row)
    for d in far_first:
        ag_copies[d].wait_recv()
        mixed = mixed + mix(lax.rem(my_row + n_row - d, n_row))
    update = (gate * mixed.reshape(flat, C)).astype(bf16)
    pair = (pair.astype(f32) + dot(update, out_ref[1])).astype(bf16)
    pair_out_ref[...] = pair.reshape(rows, cols, C)

    normed = layer_norm(pair, bias_gain_ref[...]).astype(bf16).reshape(rows, cols, C)
    bias = [dot_nt(bias_proj_ref[...], normed[i]) for i in range(rows)]
    scores = scores + jnp.concatenate(bias, axis=0).astype(bf16).astype(f32)
    weights = jnp.where(real, jnp.exp(cap_value * jnp.tanh(scores * (1.0 / cap_value))), 0.0)
    bottom = jnp.sum(weights, axis=1, keepdims=True)
    weights = weights.astype(bf16)
    diagonal = iota((heads, C), 0) == iota((heads, C), 1)
    bottom = jnp.sum(jnp.where(diagonal[None], bottom.reshape(rows, heads, 1), 0.0), axis=1)
    bottom_high = bottom.astype(bf16)
    den_send[:, :C] = bottom_high
    den_send[:, C:] = (bottom - bottom_high.astype(f32)).astype(bf16)
    tops = []
    for c in range(n_col):
        attended = dot(weights, kv_own[c, :, 1].reshape(cols, width)).reshape(rows, heads, width)
        tops.append(jnp.sum(jnp.where(lanes_of[c][None], attended, 0.0), axis=1))
        num_send[c] = tops[c].astype(bf16)
    den_copies = push_cols(lambda d: den_send, lambda d: den_recv.at[d - 1], den_send_sem, den_recv_sem)
    num_copies = push_cols(lambda d: num_send, lambda d: num_recv.at[d - 1], num_send_sem, num_recv_sem)
    for copy in aout_copies:
        copy.wait_recv()
    deep = iota((2 * C, width), 0) & (C - 1)
    flat_lane = iota((2 * C, width), 1)
    wide_of = []
    for c in range(n_col):
        start = (deep - c * heads_here) * HEAD_DIM
        wide_of.append(((flat_lane >= start) & (flat_lane < start + HEAD_DIM)).astype(f32).astype(bf16))
    for d in range(1, n_col):
        den_copies[d - 1].wait_recv()
        bottom = bottom + (den_recv[d - 1, :, :C].astype(f32) + den_recv[d - 1, :, C:].astype(f32))
    inverse = jnp.where(iota((rows, C), 1) < heads, 1.0 / bottom, 0.0)
    inverse_high = inverse.astype(bf16)
    inverse = jnp.concatenate([inverse_high, (inverse - inverse_high.astype(f32)).astype(bf16)], axis=1)
    factors = [query_gates[c, 1].astype(f32) * dot(inverse, wide_of[c]) for c in range(n_col)]
    for copy in num_copies:
        copy.wait_recv()
    result = jnp.zeros((rows, width), f32)
    for c in range(n_col):
        top = tops[c]
        for d in range(1, n_col):
            top = top + num_recv[d - 1, c].astype(f32)
        result = result + dot((factors[c] * top).astype(bf16), aout_full[c])
    token_ref[...] = result.astype(bf16)
    for copy in pushed:
        copy.wait_send()


def on_device(n_row, n_col, pair_act, single, token_mask, chain_index, residue_index, tri_gain, tri_qk,
              tri_vg, tri_out, bias_gain, bias_proj, chain_bias, pos_slope, attn_gain, attn_qk, attn_vg,
              attn_out):
    rows, cols, _ = pair_act.shape
    width = attn_qk.shape[2]
    share = TRI_DIM // n_row
    per = cols // rows
    by_col = [pltpu.SemaphoreType.DMA((n_col - 1,))] * 2
    by_row = [pltpu.SemaphoreType.DMA((n_row - 1,))] * 2
    vmem = pl.BlockSpec(memory_space=pltpu.VMEM)
    anywhere = pl.BlockSpec(memory_space=pl.ANY)
    return pl.pallas_call(
        functools.partial(kernel, n_row, n_col),
        out_shape=(
            jax.ShapeDtypeStruct(pair_act.shape, bf16),
            jax.ShapeDtypeStruct((rows, width), bf16),
        ),
        in_specs=[vmem] * 14 + [anywhere] * 3,
        out_specs=(vmem, vmem),
        scratch_shapes=[
            pltpu.VMEM((2, width) + attn_qk.shape[1:2], bf16),
            pltpu.VMEM((2, width) + attn_vg.shape[1:2], bf16),
            pltpu.VMEM(attn_out.shape, bf16),
            pltpu.VMEM((rows, TRI_DIM, C), bf16),
            pltpu.VMEM((n_col - 1, rows, TRI_DIM, C), bf16),
            pltpu.VMEM((n_row, share, cols, C), bf16),
            pltpu.VMEM((n_row - 1, share, cols, C), bf16),
            pltpu.VMEM((n_row, share, cols, C), bf16),
            pltpu.VMEM((TRI_DIM, rows * cols, C), bf16),
            pltpu.VMEM((n_row, 2, rows, width), bf16),
            pltpu.VMEM((n_col, per, 2, rows, width), bf16),
            pltpu.VMEM((n_col, 2, rows, width), bf16),
            pltpu.VMEM((n_col, 8, C), f32),
            pltpu.VMEM((n_col, width, width), bf16),
            pltpu.VMEM((n_col, width, width), bf16),
            pltpu.VMEM((n_col, rows, width), bf16),
            pltpu.VMEM((n_col - 1, n_col, rows, width), bf16),
            pltpu.VMEM((rows, 2 * C), bf16),
            pltpu.VMEM((n_col - 1, rows, 2 * C), bf16),
            pltpu.SemaphoreType.DMA((3,)),
        ] + by_col + by_row + by_row + by_row + by_col * 6,
        compiler_params=pltpu.CompilerParams(
            collective_id=0, has_side_effects=True, vmem_limit_bytes=50 * 1024 * 1024
        ),
    )(
        pair_act, single, token_mask.reshape(1, -1), chain_index.reshape(1, -1),
        residue_index.reshape(1, -1), tri_gain, tri_qk, tri_vg, tri_out, bias_gain.reshape(1, -1),
        bias_proj.T, chain_bias.reshape(1, -1), pos_slope.reshape(1, -1), attn_gain.reshape(1, -1),
        jnp.swapaxes(attn_qk, 1, 2), jnp.swapaxes(attn_vg, 1, 2), attn_out,
    )


def solution(mesh):
    return jax.shard_map(
        functools.partial(on_device, mesh.shape["row"], mesh.shape["col"]),
        mesh=mesh,
        in_specs=(
            P(("grp", "row"), "col", None),
            P(("grp", "row"), None),
            P("grp"),
            P("grp"),
            P("grp"),
            P(),
            P(),
            P(),
            P(),
            P(),
            P(),
            P("col"),
            P("col"),
            P(),
            P(None, None, "col"),
            P(None, None, "col"),
            P("col", None),
        ),
        out_specs=(P(("grp", "row"), "col", None), P(("grp", "row"), "col")),
        check_vma=False,
    )
```

profile of v0, /device:TPU:0, one launch (start us, length us, event | category | flops | bytes accessed | tf_op | source)
XLA Modules:
  0.0 41.6 jit_solution(18441159435001077114)
XLA Ops:
  0.6 0.0 copy-start.7
  0.6 0.7 %reshape.31.attn_gain_ref = f32[1,768]{1,0:T(1,128)S(1)} reshape(f32[768]{0:T(1024)} %param.30) | data formatting | bytes 6144 | tf_op jit(solution)/shard_map/reshape | solution.py:423
  1.3 0.0 copy-done.7
  1.4 0.0 copy-start
  1.4 1.1 %copy-done = bf16[2,768,192]{1,2,0:T(8,128)(2,1)S(1)} copy-done((bf16[2,768,192]{1,2,0:T(8,128)(2,1)S(1)}, bf16[2,768,192]{1,2,0:T(8,128)(2,1)}, u32[]{:S(2)}) %copy-start) | copy-done | bytes 589848
  2.4 0.0 copy-start.1
  2.4 1.1 %copy-done.1 = bf16[2,768,192]{1,2,0:T(8,128)(2,1)S(1)} copy-done((bf16[2,768,192]{1,2,0:T(8,128)(2,1)S(1)}, bf16[2,768,192]{1,2,0:T(8,128)(2,1)}, u32[]{:S(2)}) %copy-start.1) | copy-done | bytes 589848
  3.5 0.0 copy-start.2
  3.5 1.0 %copy-done.2 = bf16[192,768]{1,0:T(8,128)(2,1)S(1)} copy-done((bf16[192,768]{1,0:T(8,128)(2,1)S(1)}, bf16[192,768]{1,0:T(8,128)(2,1)}, u32[]{:S(2)}) %copy-start.2) | copy-done | bytes 294936
  4.5 0.0 copy-start.3
  4.5 0.9 %copy-done.3 = bf16[16,32,128]{2,1,0:T(8,128)(2,1)S(1)} copy-done((bf16[16,32,128]{2,1,0:T(8,128)(2,1)S(1)}, bf16[16,32,128]{2,1,0:T(8,128)(2,1)}, u32[]{:S(2)}) %copy-start.3) | copy-done | bytes 131096
  5.4 0.0 copy-start.4
  5.4 0.9 %copy-done.4 = bf16[2,128,256]{2,1,0:T(8,128)(2,1)S(1)} copy-done((bf16[2,128,256]{2,1,0:T(8,128)(2,1)S(1)}, bf16[2,128,256]{2,1,0:T(8,128)(2,1)}, u32[]{:S(2)}) %copy-start.4) | copy-done | bytes 131096
  6.3 0.0 copy-start.5
  6.3 0.9 %copy-done.5 = bf16[2,128,256]{2,1,0:T(8,128)(2,1)S(1)} copy-done((bf16[2,128,256]{2,1,0:T(8,128)(2,1)S(1)}, bf16[2,128,256]{2,1,0:T(8,128)(2,1)}, u32[]{:S(2)}) %copy-start.5) | copy-done | bytes 131096
  7.2 0.0 copy-start.6
  7.2 0.8 %copy-done.6 = bf16[2,128,128]{2,1,0:T(8,128)(2,1)S(1)} copy-done((bf16[2,128,128]{2,1,0:T(8,128)(2,1)S(1)}, bf16[2,128,128]{2,1,0:T(8,128)(2,1)}, u32[]{:S(2)}) %copy-start.6) | copy-done | bytes 65560
  8.0 0.0 copy-start.8
  8.0 0.7 %copy-done.8 = bf16[128,16]{0,1:T(8,128)(2,1)S(1)} copy-done((bf16[128,16]{0,1:T(8,128)(2,1)S(1)}, bf16[128,16]{0,1:T(8,128)(2,1)}, u32[]{:S(2)}) %copy-start.8) | copy-done | bytes 4120
  8.7 0.0 copy-start.9
  8.7 0.7 %copy-done.9 = f32[2,128]{1,0:T(2,128)S(1)} copy-done((f32[2,128]{1,0:T(2,128)S(1)}, f32[2,128]{1,0:T(2,128)}, u32[]{:S(2)}) %copy-start.9) | copy-done | bytes 1048
  9.4 0.0 copy-start.10
  9.4 0.7 %copy-done.10 = s32[128]{0:T(128)S(1)} copy-done((s32[128]{0:T(128)S(1)}, s32[128]{0:T(128)}, u32[]{:S(2)}) %copy-start.10) | copy-done | bytes 536
  10.0 0.0 copy-start.11
  10.0 0.7 %copy-done.11 = s32[128]{0:T(128)S(1)} copy-done((s32[128]{0:T(128)S(1)}, s32[128]{0:T(128)}, u32[]{:S(2)}) %copy-start.11) | copy-done | bytes 536
  10.7 0.7 %copy-done.12 = s32[128]{0:T(128)S(1)} copy-done((s32[128]{0:T(128)S(1)}, s32[128]{0:T(128)}, u32[]{:S(2)}) %copy-start.12) | copy-done | bytes 536
  11.4 0.7 %copy-done.13 = f32[128]{0:T(128)S(1)} copy-done((f32[128]{0:T(128)S(1)}, f32[128]{0:T(128)}, u32[]{:S(2)}) %copy-start.13) | copy-done | bytes 536
  12.0 0.7 %copy-done.14 = f32[4]{0:T(128)S(1)} copy-done((f32[4]{0:T(128)S(1)}, f32[4]{0:T(128)}, u32[]{:S(2)}) %copy-start.14) | copy-done | bytes 40
  12.7 0.7 %copy-done.15 = f32[4]{0:T(128)S(1)} copy-done((f32[4]{0:T(128)S(1)}, f32[4]{0:T(128)}, u32[]{:S(2)}) %copy-start.15) | copy-done | bytes 40
  13.3 27.0 %shard_map.176 = (bf16[16,32,128]{2,1,0:T(8,128)(2,1)S(1)}, bf16[16,192]{1,0:T(8,128)(2,1)S(1)}) custom-call(bf16[16,32,128]{2,1,0:T(8,128)(2,1)S(1)} %copy-done.3, bf16[16,768]{1,0:T(8,128)(2,1)S(1)} %copy-done.7, s32[1,128]{1,0:T(1,128)S(1)} %bitcast.12, s32[1,128]{1,0:T(1,128)S(1)} %bitcast.13, s32[1,128]{1,0:T(1,128)S(1)} %bitcast.14, ...), custom_call_target="tpu_custom_call" | custom-call | tf_op jit(solution)/shard_map/pallas_call | solution.py:387
  40.4 0.7 %copy.21 = bf16[16,32,128]{2,1,0:T(8,128)(2,1)} copy(bf16[16,32,128]{2,1,0:T(8,128)(2,1)S(1)} %get-tuple-element.4) | data formatting | bytes 262144
  41.0 0.6 %copy.22 = bf16[16,192]{1,0:T(8,128)(2,1)} copy(bf16[16,192]{1,0:T(8,128)(2,1)S(1)} %get-tuple-element.5) | data formatting | bytes 12288
  (4 shorter events, 0.0 us)
Async XLA Ops:
  0.6 0.7 %copy-start.7 = (bf16[16,768]{1,0:T(8,128)(2,1)S(1)}, bf16[16,768]{1,0:T(8,128)(2,1)}, u32[]{:S(2)}) copy-start(bf16[16,768]{1,0:T(8,128)(2,1)} %single_ref.1) | copy-start | bytes 73732
  1.4 1.1 %copy-start = (bf16[2,768,192]{1,2,0:T(8,128)(2,1)S(1)}, bf16[2,768,192]{1,2,0:T(8,128)(2,1)}, u32[]{:S(2)}) copy-start(bf16[2,768,192]{1,2,0:T(8,128)(2,1)} %param.31) | copy-start | bytes 1769476
  2.4 1.1 %copy-start.1 = (bf16[2,768,192]{1,2,0:T(8,128)(2,1)S(1)}, bf16[2,768,192]{1,2,0:T(8,128)(2,1)}, u32[]{:S(2)}) copy-start(bf16[2,768,192]{1,2,0:T(8,128)(2,1)} %param.32) | copy-start | bytes 1769476
  3.5 1.0 %copy-start.2 = (bf16[192,768]{1,0:T(8,128)(2,1)S(1)}, bf16[192,768]{1,0:T(8,128)(2,1)}, u32[]{:S(2)}) copy-start(bf16[192,768]{1,0:T(8,128)(2,1)} %aout_hbm.1) | copy-start | bytes 884740
  4.5 0.9 %copy-start.3 = (bf16[16,32,128]{2,1,0:T(8,128)(2,1)S(1)}, bf16[16,32,128]{2,1,0:T(8,128)(2,1)}, u32[]{:S(2)}) copy-start(bf16[16,32,128]{2,1,0:T(8,128)(2,1)} %pair_ref.1) | copy-start | bytes 393220
  5.4 0.9 %copy-start.4 = (bf16[2,128,256]{2,1,0:T(8,128)(2,1)S(1)}, bf16[2,128,256]{2,1,0:T(8,128)(2,1)}, u32[]{:S(2)}) copy-start(bf16[2,128,256]{2,1,0:T(8,128)(2,1)} %qk_ref.1) | copy-start | bytes 393220
  6.3 0.9 %copy-start.5 = (bf16[2,128,256]{2,1,0:T(8,128)(2,1)S(1)}, bf16[2,128,256]{2,1,0:T(8,128)(2,1)}, u32[]{:S(2)}) copy-start(bf16[2,128,256]{2,1,0:T(8,128)(2,1)} %vg_ref.1) | copy-start | bytes 393220
  7.2 0.8 %copy-start.6 = (bf16[2,128,128]{2,1,0:T(8,128)(2,1)S(1)}, bf16[2,128,128]{2,1,0:T(8,128)(2,1)}, u32[]{:S(2)}) copy-start(bf16[2,128,128]{2,1,0:T(8,128)(2,1)} %out_ref.1) | copy-start | bytes 196612
  8.0 0.7 %copy-start.8 = (bf16[128,16]{0,1:T(8,128)(2,1)S(1)}, bf16[128,16]{0,1:T(8,128)(2,1)}, u32[]{:S(2)}) copy-start(bf16[128,16]{0,1:T(8,128)(2,1)} %param.27) | copy-start | bytes 12292
  8.7 0.7 %copy-start.9 = (f32[2,128]{1,0:T(2,128)S(1)}, f32[2,128]{1,0:T(2,128)}, u32[]{:S(2)}) copy-start(f32[2,128]{1,0:T(2,128)} %gain_ref.1) | copy-start | bytes 3076
  9.4 0.7 %copy-start.10 = (s32[128]{0:T(128)S(1)}, s32[128]{0:T(128)}, u32[]{:S(2)}) copy-start(s32[128]{0:T(128)} %param.19) | copy-start | bytes 1540
  10.0 0.7 %copy-start.11 = (s32[128]{0:T(128)S(1)}, s32[128]{0:T(128)}, u32[]{:S(2)}) copy-start(s32[128]{0:T(128)} %param.20) | copy-start | bytes 1540
  10.7 0.7 %copy-start.12 = (s32[128]{0:T(128)S(1)}, s32[128]{0:T(128)}, u32[]{:S(2)}) copy-start(s32[128]{0:T(128)} %param.21) | copy-start | bytes 1540
  11.3 0.7 %copy-start.13 = (f32[128]{0:T(128)S(1)}, f32[128]{0:T(128)}, u32[]{:S(2)}) copy-start(f32[128]{0:T(128)} %param.26) | copy-start | bytes 1540
  12.0 0.7 %copy-start.14 = (f32[4]{0:T(128)S(1)}, f32[4]{0:T(128)}, u32[]{:S(2)}) copy-start(f32[4]{0:T(128)} %param.28) | copy-start | bytes 52
  12.7 0.7 %copy-start.15 = (f32[4]{0:T(128)S(1)}, f32[4]{0:T(128)}, u32[]{:S(2)}) copy-start(f32[4]{0:T(128)} %param.29) | copy-start | bytes 52
where the time goes:
time: 42.1 us; the launch traced here: 41.6 us
  Pallas kernels  27 us (64%)
  local copies, waits for them, and re-layouts  13.9 us (33%)
  between operations  0.66 us (2%)
    pallas_call x1, Pallas kernels, on_device(): pl.pallas_call(functools.partial(kernel, n_row, n_col), out_shape=(jax.Sh...  27 us
    unnamed x34, local copies, waits for them, and re-layouts  13.2 us

commit v1 on v0

--- a/solution.py
+++ b/solution.py
@@ -61,6 +61,26 @@
 def kernel(
     n_row,
     n_col,
+    pair_hbm,
+    single_hbm,
+    mask_hbm,
+    chain_hbm,
+    residue_hbm,
+    gain_hbm,
+    qk_hbm,
+    vg_hbm,
+    out_hbm,
+    bias_gain_hbm,
+    bias_proj_hbm,
+    chain_bias_hbm,
+    slope_hbm,
+    attn_gain_hbm,
+    aqk_hbm,
+    avg_hbm,
+    aout_hbm,
+    pair_out_hbm,
+    token_ref,
+    pair_out_ref,
     pair_ref,
     single_ref,
     mask_ref,
@@ -75,11 +95,6 @@
     chain_bias_ref,
     slope_ref,
     attn_gain_ref,
-    aqk_hbm,
-    avg_hbm,
-    aout_hbm,
-    pair_out_ref,
-    token_ref,
     aqk_ref,
     avg_ref,
     aout_ref,
@@ -100,6 +115,7 @@
     den_send,
     den_recv,
     load_sem,
+    store_sem,
     row_send_sem,
     row_recv_sem,
     rs_send_sem,
@@ -158,11 +174,22 @@
         pl.semaphore_signal(barrier, inc=1, device_id={"col": col_peers[d]}, device_id_type=MESH)
     for d in range(1, n_row):
         pl.semaphore_signal(barrier, inc=1, device_id={"row": row_peers[d]}, device_id_type=MESH)
-    loads = []
-    for position, (src, dst) in enumerate(((aqk_hbm, aqk_ref), (avg_hbm, avg_ref), (aout_hbm, aout_ref))):
-        loads.append(pltpu.make_async_copy(src, dst, load_sem.at[position]))
-        loads[-1].start()
-
+    loads = {}
+    for position, (src, dst) in enumerate((
+        (pair_hbm, pair_ref), (gain_hbm, gain_ref), (qk_hbm, qk_ref), (vg_hbm, vg_ref), (mask_hbm, mask_ref),
+        (single_hbm, single_ref), (attn_gain_hbm, attn_gain_ref), (chain_bias_hbm, chain_bias_ref),
+        (slope_hbm, slope_ref), (aqk_hbm, aqk_ref), (avg_hbm, avg_ref), (out_hbm, out_ref), (aout_hbm, aout_ref),
+        (chain_hbm, chain_ref), (residue_hbm, residue_ref), (bias_gain_hbm, bias_gain_ref),
+        (bias_proj_hbm, bias_proj_ref),
+    )):
+        loads[id(dst)] = pltpu.make_async_copy(src, dst, load_sem.at[position])
+        loads[id(dst)].start()
+
+    def loaded(*refs):
+        for ref in refs:
+            loads[id(ref)].wait()
+
+    loaded(pair_ref, gain_ref, qk_ref, vg_ref, mask_ref)
     length = jnp.sum(mask_ref[...].astype(f32), axis=1, keepdims=True)
 
     pair = pair_ref[...].reshape(flat, C)
@@ -182,6 +209,7 @@
     pl.semaphore_wait(barrier, n_row + n_col - 2)
     row_copies = push_cols(lambda d: row_part, lambda d: row_recv.at[d - 1], row_send_sem, row_recv_sem)
 
+    loaded(single_ref, attn_gain_ref, chain_bias_ref, slope_ref)
     lane = iota((8, C), 1)
     top = iota((8, C), 0) == 0
     relation = jnp.zeros((8, C), f32)
@@ -190,9 +218,9 @@
         relation = relation + jnp.where(lane == my_col * heads_here + h, pick, 0.0)
     rel[my_col] = relation
     rel_copies = push_cols(lambda d: rel.at[my_col], lambda d: rel.at[my_col], rel_send_sem, rel_recv_sem)
-    tok = layer_norm(single_ref[...], attn_gain_ref[...]).astype(bf16)
-    loads[0].wait()
-    loads[1].wait()
+    gains = [attn_gain_ref[g:g + 1, :] for g in range(attn_gain_ref.shape[0])]
+    tok = layer_norm(single_ref[...], jnp.concatenate(gains, axis=1)).astype(bf16)
+    loaded(aqk_ref, avg_ref)
     kv[my_row, 0] = dot_nt(tok, aqk_ref[1]).astype(bf16)
     kv[my_row, 1] = dot_nt(tok, avg_ref[0]).astype(bf16)
     kv_copies = {}
@@ -204,11 +232,12 @@
     gate = sigmoid(query_gate[:, C:]) * tri_scale
     query_gates[my_col, 0] = dot_nt(tok, aqk_ref[0]).astype(bf16)
     query_gates[my_col, 1] = sigmoid(dot_nt(tok, avg_ref[1])).astype(bf16)
-    loads[2].wait()
+    loaded(aout_ref)
     for c in range(n_col):
         aout_send[c] = aout_ref[:, c * width:(c + 1) * width]
     aout_full[my_col] = aout_send[my_col]
 
+    loaded(out_ref, chain_ref, residue_ref, bias_gain_ref, bias_proj_ref)
     for copy in row_copies:
         copy.wait_recv()
     qg_copies = push_cols(lambda d: query_gates.at[my_col], lambda d: query_gates.at[my_col],
@@ -326,6 +355,8 @@
     update = (gate * mixed.reshape(flat, C)).astype(bf16)
     pair = (pair.astype(f32) + dot(update, out_ref[1])).astype(bf16)
     pair_out_ref[...] = pair.reshape(rows, cols, C)
+    store = pltpu.make_async_copy(pair_out_ref, pair_out_hbm, store_sem)
+    store.start()
 
     normed = layer_norm(pair, bias_gain_ref[...]).astype(bf16).reshape(rows, cols, C)
     bias = [dot_nt(bias_proj_ref[...], normed[i]) for i in range(rows)]
@@ -369,6 +400,7 @@
             top = top + num_recv[d - 1, c].astype(f32)
         result = result + dot((factors[c] * top).astype(bf16), aout_full[c])
     token_ref[...] = result.astype(bf16)
+    store.wait()
     for copy in pushed:
         copy.wait_send()
 
@@ -383,19 +415,21 @@
     by_col = [pltpu.SemaphoreType.DMA((n_col - 1,))] * 2
     by_row = [pltpu.SemaphoreType.DMA((n_row - 1,))] * 2
     vmem = pl.BlockSpec(memory_space=pltpu.VMEM)
-    anywhere = pl.BlockSpec(memory_space=pl.ANY)
+    inputs = (
+        pair_act, single, token_mask.reshape(1, -1), chain_index.reshape(1, -1),
+        residue_index.reshape(1, -1), tri_gain, tri_qk, tri_vg, tri_out, bias_gain.reshape(1, -1),
+        bias_proj.T, chain_bias.reshape(1, -1), pos_slope.reshape(1, -1), attn_gain.reshape(-1, C),
+        jnp.swapaxes(attn_qk, 1, 2), jnp.swapaxes(attn_vg, 1, 2), attn_out,
+    )
     return pl.pallas_call(
         functools.partial(kernel, n_row, n_col),
         out_shape=(
             jax.ShapeDtypeStruct(pair_act.shape, bf16),
             jax.ShapeDtypeStruct((rows, width), bf16),
         ),
-        in_specs=[vmem] * 14 + [anywhere] * 3,
-        out_specs=(vmem, vmem),
-        scratch_shapes=[
-            pltpu.VMEM((2, width) + attn_qk.shape[1:2], bf16),
-            pltpu.VMEM((2, width) + attn_vg.shape[1:2], bf16),
-            pltpu.VMEM(attn_out.shape, bf16),
+        in_specs=[pl.BlockSpec(memory_space=pltpu.HBM)] * 17,
+        out_specs=(pl.BlockSpec(memory_space=pltpu.HBM), vmem),
+        scratch_shapes=[pltpu.VMEM(value.shape, value.dtype) for value in inputs[:1] + inputs] + [
             pltpu.VMEM((rows, TRI_DIM, C), bf16),
             pltpu.VMEM((n_col - 1, rows, TRI_DIM, C), bf16),
             pltpu.VMEM((n_row, share, cols, C), bf16),
@@ -412,17 +446,13 @@
             pltpu.VMEM((n_col - 1, n_col, rows, width), bf16),
             pltpu.VMEM((rows, 2 * C), bf16),
             pltpu.VMEM((n_col - 1, rows, 2 * C), bf16),
-            pltpu.SemaphoreType.DMA((3,)),
+            pltpu.SemaphoreType.DMA((len(inputs),)),
+            pltpu.SemaphoreType.DMA,
         ] + by_col + by_row + by_row + by_row + by_col * 6,
         compiler_params=pltpu.CompilerParams(
-            collective_id=0, has_side_effects=True, vmem_limit_bytes=50 * 1024 * 1024
+            collective_id=0, has_side_effects=True, vmem_limit_bytes=64 * 1024 * 1024
         ),
-    )(
-        pair_act, single, token_mask.reshape(1, -1), chain_index.reshape(1, -1),
-        residue_index.reshape(1, -1), tri_gain, tri_qk, tri_vg, tri_out, bias_gain.reshape(1, -1),
-        bias_proj.T, chain_bias.reshape(1, -1), pos_slope.reshape(1, -1), attn_gain.reshape(1, -1),
-        jnp.swapaxes(attn_qk, 1, 2), jnp.swapaxes(attn_vg, 1, 2), attn_out,
-    )
+    )(*inputs)
 
 
 def solution(mesh):

time: 42.1 us -> 30.8 us (0.73)
  local copies, waits for them, and re-layouts: 13.9 us -> 2.18 us
  Pallas kernels: 27 us -> 27.8 us
    unnamed x34 -> x4, local copies, waits for them, and re-layouts: 13.2 us -> 2.18 us
    pallas_call x1, Pallas kernels: 27 us -> 27.8 us  [on_device(): pl.pallas_call(functools.partial(kernel, n_row, n_col), out_shape=(jax.Sh...]
    reshape x1 -> x0, local copies, waits for them, and re-layouts: 0.7 us -> none  [on_device(): attn_gain.reshape(1, -1)]
where the time goes in v1:
time: 30.8 us; the launch traced here: 30.6 us
  Pallas kernels  27.8 us (90%)
  local copies, waits for them, and re-layouts  2.18 us (7%)
  between operations  0.65 us (2%)
    pallas_call x1, Pallas kernels, on_device(): pl.pallas_call(functools.partial(kernel, n_row, n_col), out_shape=(jax.Sh...  27.8 us
    unnamed x4, local copies, waits for them, and re-layouts  2.18 us

profile of v1, /device:TPU:0, one launch (start us, length us, event | category | flops | bytes accessed | tf_op | source)
XLA Modules:
  0.0 30.6 jit_solution(10852855801212216663)
XLA Ops:
  0.6 27.8 %shard_map.176 = (bf16[16,32,128]{2,1,0:T(8,128)(2,1)}, bf16[16,192]{1,0:T(8,128)(2,1)}) custom-call(bf16[16,32,128]{2,1,0:T(8,128)(2,1)} %pair_hbm.1, bf16[16,768]{1,0:T(8,128)(2,1)} %single_hbm.1, s32[1,128]{1,0:T(1,128)} %bitcast.14, s32[1,128]{1,0:T(1,128)} %bitcast.15, s32[1,128]{1,0:T(1,128)} %bitcast.16, f32[2,128]{1,0:T(2,128)} %gain_hbm.1, ...), custom_call_target="tpu_custom_call" | custom-call | tf_op jit(solution)/shard_map/pallas_call | solution.py:424
  28.5 0.0 copy-start
  28.5 1.6 %copy.21 = bf16[16,32,128]{2,1,0:T(8,128)(2,1)} copy(bf16[16,32,128]{2,1,0:T(8,128)(2,1)} %get-tuple-element.4) | data formatting | bytes 262144
  30.0 0.0 copy-done
  30.0 0.6 %copy.22 = bf16[16,192]{1,0:T(8,128)(2,1)} copy(bf16[16,192]{1,0:T(8,128)(2,1)S(1)} %copy-done) | data formatting | bytes 12288
Async XLA Ops:
  28.5 1.6 %copy-start = (bf16[16,192]{1,0:T(8,128)(2,1)S(1)}, bf16[16,192]{1,0:T(8,128)(2,1)}, u32[]{:S(2)}) copy-start(bf16[16,192]{1,0:T(8,128)(2,1)} %get-tuple-element.5) | copy-start | bytes 18436

commit v2 on v1

--- a/solution.py
+++ b/solution.py
@@ -164,16 +164,12 @@
         return copy
 
     def push_cols(src_of, dst_of, send_sem, recv_sem):
-        return [
-            push(src_of(d), dst_of(d), send_sem.at[d - 1], recv_sem.at[d - 1], {"col": col_peers[d]})
-            for d in range(1, n_col)
-        ]
-
-    barrier = pltpu.get_barrier_semaphore()
-    for d in range(1, n_col):
-        pl.semaphore_signal(barrier, inc=1, device_id={"col": col_peers[d]}, device_id_type=MESH)
-    for d in range(1, n_row):
-        pl.semaphore_signal(barrier, inc=1, device_id={"row": row_peers[d]}, device_id_type=MESH)
+        copies = {
+            d: push(src_of(d), dst_of(d), send_sem.at[d - 1], recv_sem.at[d - 1], {"col": col_peers[d]})
+            for d in sorted(range(1, n_col), key=lambda d: abs(2 * d - n_col))
+        }
+        return [copies[d] for d in range(1, n_col)]
+
     loads = {}
     for position, (src, dst) in enumerate((
         (pair_hbm, pair_ref), (gain_hbm, gain_ref), (qk_hbm, qk_ref), (vg_hbm, vg_ref), (mask_hbm, mask_ref),
@@ -189,25 +185,38 @@
         for ref in refs:
             loads[id(ref)].wait()
 
+    barrier = pltpu.get_barrier_semaphore()
+    for d in range(1, n_col):
+        pl.semaphore_signal(barrier, inc=1, device_id={"col": col_peers[d]}, device_id_type=MESH)
+    for d in range(1, n_row):
+        pl.semaphore_signal(barrier, inc=1, device_id={"row": row_peers[d]}, device_id_type=MESH)
     loaded(pair_ref, gain_ref, qk_ref, vg_ref, mask_ref)
     length = jnp.sum(mask_ref[...].astype(f32), axis=1, keepdims=True)
 
-    pair = pair_ref[...].reshape(flat, C)
-    normed = layer_norm(pair, gain_ref[0:1, :]).astype(bf16)
-    key_value = dot(normed, jnp.concatenate([qk_ref[0, :, C:], vg_ref[0, :, :C]], axis=1))
+    half = rows // 2
     col_pos = (iota((1, cols, C), 1) + col_first).astype(f32)
     col_keep = col_pos < length.reshape(1, 1, 1)
-    key_feat = jnp.where(col_keep, feature(key_value[:, :C]).reshape(rows, cols, C), 0.0).astype(bf16)
-    values = key_value[:, C:].astype(bf16).reshape(rows, cols, C)
     dim_shift = log2(TRI_DIM)
     left = iota((C, C), 0)
     right = iota((C, C), 1)
     same_head = (left >> dim_shift) == (right >> dim_shift)
-    for i in range(rows):
-        outer = jnp.where(same_head, dot_tn(key_feat[i], values[i]), 0.0)
-        row_part[i] = jnp.sum(outer.reshape(TRI_HEADS, TRI_DIM, C), axis=0).astype(bf16)
-    pl.semaphore_wait(barrier, n_row + n_col - 2)
-    row_copies = push_cols(lambda d: row_part, lambda d: row_recv.at[d - 1], row_send_sem, row_recv_sem)
+    key_value_weight = jnp.concatenate([qk_ref[0, :, C:], vg_ref[0, :, :C]], axis=1)
+    normed_halves = []
+    row_copies = []
+    for b in range(2):
+        part = pair_ref[b * half:(b + 1) * half].reshape(half * cols, C)
+        normed_halves.append(layer_norm(part, gain_ref[0:1, :]).astype(bf16))
+        key_value = dot(normed_halves[b], key_value_weight)
+        key_feat = jnp.where(col_keep, feature(key_value[:, :C]).reshape(half, cols, C), 0.0).astype(bf16)
+        values = key_value[:, C:].astype(bf16).reshape(half, cols, C)
+        for i in range(half):
+            outer = jnp.where(same_head, dot_tn(key_feat[i], values[i]), 0.0)
+            row_part[b * half + i] = jnp.sum(outer.reshape(TRI_HEADS, TRI_DIM, C), axis=0).astype(bf16)
+        if b == 0:
+            pl.semaphore_wait(barrier, n_row + n_col - 2)
+        lines = pl.ds(b * half, half)
+        row_copies.append(push_cols(lambda d: row_part.at[lines], lambda d: row_recv.at[d - 1, lines],
+                                    row_send_sem.at[b], row_recv_sem.at[b]))
 
     loaded(single_ref, attn_gain_ref, chain_bias_ref, slope_ref)
     lane = iota((8, C), 1)
@@ -227,9 +236,13 @@
     for d in far_first:
         kv_copies[d] = push(kv.at[my_row], kv.at[my_row], kv_send_sem.at[d - 1],
                             kv_recv_sem.at[d - 1], {"row": row_peers[d]})
-    query_gate = dot(normed, jnp.concatenate([qk_ref[0, :, :C], vg_ref[0, :, C:]], axis=1))
-    query_feat = feature(query_gate[:, :C]).astype(bf16).reshape(rows, cols, C)
-    gate = sigmoid(query_gate[:, C:]) * tri_scale
+    query_gate_weight = jnp.concatenate([qk_ref[0, :, :C], vg_ref[0, :, C:]], axis=1)
+    feat_halves = []
+    gate_halves = []
+    for b in range(2):
+        query_gate = dot(normed_halves[b], query_gate_weight)
+        feat_halves.append(feature(query_gate[:, :C]).astype(bf16).reshape(half, cols, C))
+        gate_halves.append(sigmoid(query_gate[:, C:]) * tri_scale)
     query_gates[my_col, 0] = dot_nt(tok, aqk_ref[0]).astype(bf16)
     query_gates[my_col, 1] = sigmoid(dot_nt(tok, avg_ref[1])).astype(bf16)
     loaded(aout_ref)
@@ -238,30 +251,36 @@
     aout_full[my_col] = aout_send[my_col]
 
     loaded(out_ref, chain_ref, residue_ref, bias_gain_ref, bias_proj_ref)
-    for copy in row_copies:
-        copy.wait_recv()
+    key_value_weight = jnp.concatenate([qk_ref[1, :, C:], vg_ref[1, :, :C]], axis=1)
+    pairs, normed, key_feat, values = [], [], [], []
+    for b in range(2):
+        for copy in row_copies[b]:
+            copy.wait_recv()
+        lines = slice(b * half, (b + 1) * half)
+        states = row_part[lines].astype(f32)
+        for d in range(1, n_col):
+            states = states + row_recv[d - 1, lines].astype(f32)
+        states = states.astype(bf16)
+        mixed = []
+        for i in range(half):
+            block = jnp.concatenate([states[i]] * TRI_HEADS, axis=0)
+            block = jnp.where(same_head, block, jnp.zeros_like(block))
+            mixed.append(dot(feat_halves[b][i], block))
+        update = (gate_halves[b] * jnp.concatenate(mixed, axis=0)).astype(bf16)
+        part = pair_ref[lines].reshape(half * cols, C).astype(f32)
+        pairs.append((part + dot(update, out_ref[0])).astype(bf16))
+        normed.append(layer_norm(pairs[b], gain_ref[1:2, :]).astype(bf16))
+        key_value = dot(normed[b], key_value_weight)
+        row_pos = (iota((half, 1, C), 0) + row_first + b * half).astype(f32)
+        row_keep = row_pos < length.reshape(1, 1, 1)
+        feat = jnp.where(row_keep, feature(key_value[:, :C]).reshape(half, cols, C), 0.0)
+        key_feat.append(feat.astype(bf16).reshape(half * cols, C))
+        values.append(key_value[:, C:])
+    pair, normed, key_feat, values = [jnp.concatenate(both, axis=0)
+                                      for both in (pairs, normed, key_feat, values)]
     qg_copies = push_cols(lambda d: query_gates.at[my_col], lambda d: query_gates.at[my_col],
                           qg_send_sem, qg_recv_sem)
-    states = row_part[...].astype(f32)
-    for d in range(1, n_col):
-        states = states + row_recv[d - 1].astype(f32)
-    states = states.astype(bf16)
-    mixed = []
-    for i in range(rows):
-        block = jnp.concatenate([states[i]] * TRI_HEADS, axis=0)
-        block = jnp.where(same_head, block, jnp.zeros_like(block))
-        mixed.append(dot(query_feat[i], block))
-    mixed = jnp.concatenate(mixed, axis=0)
-    update = (gate * mixed).astype(bf16)
-    pair = (pair.astype(f32) + dot(update, out_ref[0])).astype(bf16)
-
-    normed = layer_norm(pair, gain_ref[1:2, :]).astype(bf16)
-    key_value = dot(normed, jnp.concatenate([qk_ref[1, :, C:], vg_ref[1, :, :C]], axis=1))
-    row_pos = (iota((rows, 1, C), 0) + row_first).astype(f32)
-    row_keep = row_pos < length.reshape(1, 1, 1)
-    key_feat = jnp.where(row_keep, feature(key_value[:, :C]).reshape(rows, cols, C), 0.0)
-    key_feat = key_feat.astype(bf16).reshape(flat, C)
-    values = key_value[:, C:]
+
     entry = jnp.where(same_head, left & (TRI_DIM - 1), -1)
     share = TRI_DIM // n_row
 
@@ -279,6 +298,11 @@
         if d:
             rs_copies[d] = push(col_part.at[owner], col_recv.at[d - 1], rs_send_sem.at[d - 1],
                                 rs_recv_sem.at[d - 1], {"row": owner})
+    for d in far_first:
+        kv_copies[d].wait_recv()
+    kv_own[my_col] = kv[pl.ds(my_col * per, per)]
+    own_copies = push_cols(lambda d: kv.at[pl.ds(col_peers[d] * per, per)], lambda d: kv_own.at[my_col],
+                           own_send_sem, own_recv_sem)
     aout_copies = push_cols(lambda d: aout_send.at[col_peers[d]], lambda d: aout_full.at[my_col],
                             aout_send_sem, aout_recv_sem)
     query_gate = dot(normed, jnp.concatenate([qk_ref[1, :, :C], vg_ref[1, :, C:]], axis=1))
@@ -288,11 +312,6 @@
         wide = dot(query_feat, spread(e, 2)).astype(bf16)
         q_wide[e] = wide[:, :C]
         q_wide[e + 1] = wide[:, C:]
-    for d in far_first:
-        kv_copies[d].wait_recv()
-    kv_own[my_col] = kv[pl.ds(my_col * per, per)]
-    own_copies = push_cols(lambda d: kv.at[pl.ds(col_peers[d] * per, per)], lambda d: kv_own.at[my_col],
-                           own_send_sem, own_recv_sem)
     total = col_part[my_row].astype(f32)
     for d in far_first:
         rs_copies[d].wait_recv()
@@ -405,6 +424,17 @@
         copy.wait_send()
 
 
+def store_kernel(pair_src, token_src, pair_dst, token_dst, sems):
+    copies = [
+        pltpu.make_async_copy(pair_src, pair_dst, sems.at[0]),
+        pltpu.make_async_copy(token_src, token_dst, sems.at[1]),
+    ]
+    for copy in copies:
+        copy.start()
+    for copy in copies:
+        copy.wait()
+
+
 def on_device(n_row, n_col, pair_act, single, token_mask, chain_index, residue_index, tri_gain, tri_qk,
               tri_vg, tri_out, bias_gain, bias_proj, chain_bias, pos_slope, attn_gain, attn_qk, attn_vg,
               attn_out):
@@ -413,6 +443,7 @@
     share = TRI_DIM // n_row
     per = cols // rows
     by_col = [pltpu.SemaphoreType.DMA((n_col - 1,))] * 2
+    by_half = [pltpu.SemaphoreType.DMA((2, n_col - 1))] * 2
     by_row = [pltpu.SemaphoreType.DMA((n_row - 1,))] * 2
     vmem = pl.BlockSpec(memory_space=pltpu.VMEM)
     inputs = (
@@ -421,12 +452,11 @@
         bias_proj.T, chain_bias.reshape(1, -1), pos_slope.reshape(1, -1), attn_gain.reshape(-1, C),
         jnp.swapaxes(attn_qk, 1, 2), jnp.swapaxes(attn_vg, 1, 2), attn_out,
     )
-    return pl.pallas_call(
+    out_shape = (jax.ShapeDtypeStruct(pair_act.shape, bf16), jax.ShapeDtypeStruct((rows, width), bf16))
+    everything = 64 * 1024 * 1024
+    results = pl.pallas_call(
         functools.partial(kernel, n_row, n_col),
-        out_shape=(
-            jax.ShapeDtypeStruct(pair_act.shape, bf16),
-            jax.ShapeDtypeStruct((rows, width), bf16),
-        ),
+        out_shape=out_shape,
         in_specs=[pl.BlockSpec(memory_space=pltpu.HBM)] * 17,
         out_specs=(pl.BlockSpec(memory_space=pltpu.HBM), vmem),
         scratch_shapes=[pltpu.VMEM(value.shape, value.dtype) for value in inputs[:1] + inputs] + [
@@ -448,11 +478,19 @@
             pltpu.VMEM((n_col - 1, rows, 2 * C), bf16),
             pltpu.SemaphoreType.DMA((len(inputs),)),
             pltpu.SemaphoreType.DMA,
-        ] + by_col + by_row + by_row + by_row + by_col * 6,
+        ] + by_half + by_row + by_row + by_row + by_col * 6,
         compiler_params=pltpu.CompilerParams(
-            collective_id=0, has_side_effects=True, vmem_limit_bytes=64 * 1024 * 1024
+            collective_id=0, has_side_effects=True, vmem_limit_bytes=everything
         ),
     )(*inputs)
+    return pl.pallas_call(
+        store_kernel,
+        out_shape=out_shape,
+        in_specs=[pl.BlockSpec(memory_space=pltpu.HBM)] * 2,
+        out_specs=[pl.BlockSpec(memory_space=pltpu.HBM)] * 2,
+        scratch_shapes=[pltpu.SemaphoreType.DMA((2,))],
+        compiler_params=pltpu.CompilerParams(vmem_limit_bytes=everything),
+    )(*results)
 
 
 def solution(mesh):

time: 30.8 us -> 33.6 us (1.091)
  Pallas kernels: 27.8 us -> 32.8 us
  local copies, waits for them, and re-layouts: 2.18 us -> 0 us
    pallas_call x1 -> x2, Pallas kernels: 27.8 us -> 32.8 us  [the longest x1 27.5 us: on_device(): pl.pallas_call(functools.partial(kernel, n_row, n_col), out_shape=out_sha...]
    unnamed x4 -> x0, local copies, waits for them, and re-layouts: 2.18 us -> none
where the time goes in v2:
time: 33.6 us; the launch traced here: 33.5 us
  Pallas kernels  32.8 us (98%)
  between operations  0.65 us (2%)
    pallas_call x1, Pallas kernels, on_device(): pl.pallas_call(functools.partial(kernel, n_row, n_col), out_shape=out_sha...  27.5 us
    pallas_call x1, Pallas kernels, on_device(): pl.pallas_call(store_kernel, out_shape=out_shape, in_specs=[pl.BlockSpec(...  5.34 us

profile of v2, /device:TPU:0, one launch (start us, length us, event | category | flops | bytes accessed | tf_op | source)
XLA Modules:
  0.0 33.5 jit_solution(16730036725344241454)
XLA Ops:
  0.6 27.5 %shard_map.176 = (bf16[16,32,128]{2,1,0:T(8,128)(2,1)}, bf16[16,192]{1,0:T(8,128)(2,1)}) custom-call(bf16[16,32,128]{2,1,0:T(8,128)(2,1)} %pair_hbm.1, bf16[16,768]{1,0:T(8,128)(2,1)} %single_hbm.1, s32[1,128]{1,0:T(1,128)} %bitcast.14, s32[1,128]{1,0:T(1,128)} %bitcast.15, s32[1,128]{1,0:T(1,128)} %bitcast.16, f32[2,128]{1,0:T(2,128)} %gain_hbm.1, ...), custom_call_target="tpu_custom_call" | custom-call | tf_op jit(solution)/shard_map/pallas_call | solution.py:457
  28.1 5.3 %shard_map.177 = (bf16[16,32,128]{2,1,0:T(8,128)(2,1)}, bf16[16,192]{1,0:T(8,128)(2,1)}) custom-call(bf16[16,32,128]{2,1,0:T(8,128)(2,1)} %get-tuple-element.4.pair_src, bf16[16,192]{1,0:T(8,128)(2,1)} %get-tuple-element.5.token_src), custom_call_target="tpu_custom_call" | custom-call | tf_op jit(solution)/shard_map/pallas_call | solution.py:486

commit v3 on v2

--- a/solution.py
+++ b/solution.py
@@ -112,8 +112,6 @@
     aout_full,
     num_send,
     num_recv,
-    den_send,
-    den_recv,
     load_sem,
     store_sem,
     row_send_sem,
@@ -134,8 +132,6 @@
     aout_recv_sem,
     num_send_sem,
     num_recv_sem,
-    den_send_sem,
-    den_recv_sem,
 ):
     my_row = lax.axis_index("row")
     my_col = lax.axis_index("col")
@@ -249,6 +245,8 @@
     for c in range(n_col):
         aout_send[c] = aout_ref[:, c * width:(c + 1) * width]
     aout_full[my_col] = aout_send[my_col]
+    aout_copies = push_cols(lambda d: aout_send.at[col_peers[d]], lambda d: aout_full.at[my_col],
+                            aout_send_sem, aout_recv_sem)
 
     loaded(out_ref, chain_ref, residue_ref, bias_gain_ref, bias_proj_ref)
     key_value_weight = jnp.concatenate([qk_ref[1, :, C:], vg_ref[1, :, :C]], axis=1)
@@ -303,8 +301,6 @@
     kv_own[my_col] = kv[pl.ds(my_col * per, per)]
     own_copies = push_cols(lambda d: kv.at[pl.ds(col_peers[d] * per, per)], lambda d: kv_own.at[my_col],
                            own_send_sem, own_recv_sem)
-    aout_copies = push_cols(lambda d: aout_send.at[col_peers[d]], lambda d: aout_full.at[my_col],
-                            aout_send_sem, aout_recv_sem)
     query_gate = dot(normed, jnp.concatenate([qk_ref[1, :, :C], vg_ref[1, :, C:]], axis=1))
     query_feat = feature(query_gate[:, :C]).astype(bf16)
     gate = sigmoid(query_gate[:, C:]) * tri_scale
@@ -383,56 +379,47 @@
     weights = jnp.where(real, jnp.exp(cap_value * jnp.tanh(scores * (1.0 / cap_value))), 0.0)
     bottom = jnp.sum(weights, axis=1, keepdims=True)
     weights = weights.astype(bf16)
-    diagonal = iota((heads, C), 0) == iota((heads, C), 1)
+    lanes = num_send.shape[2]
+    spare = lanes - width
+    diagonal = iota((heads, spare), 0) == iota((heads, spare), 1)
     bottom = jnp.sum(jnp.where(diagonal[None], bottom.reshape(rows, heads, 1), 0.0), axis=1)
-    bottom_high = bottom.astype(bf16)
-    den_send[:, :C] = bottom_high
-    den_send[:, C:] = (bottom - bottom_high.astype(f32)).astype(bf16)
+    bottom_high = bottom.astype(bf16).astype(f32)
+    extras = [bottom_high, bottom - bottom_high] + [jnp.zeros((rows, spare), f32)] * (n_col - 2)
     tops = []
     for c in range(n_col):
         attended = dot(weights, kv_own[c, :, 1].reshape(cols, width)).reshape(rows, heads, width)
         tops.append(jnp.sum(jnp.where(lanes_of[c][None], attended, 0.0), axis=1))
-        num_send[c] = tops[c].astype(bf16)
-    den_copies = push_cols(lambda d: den_send, lambda d: den_recv.at[d - 1], den_send_sem, den_recv_sem)
+        num_send[c] = jnp.concatenate([tops[c], extras[c]], axis=1).astype(bf16)
     num_copies = push_cols(lambda d: num_send, lambda d: num_recv.at[d - 1], num_send_sem, num_recv_sem)
     for copy in aout_copies:
         copy.wait_recv()
-    deep = iota((2 * C, width), 0) & (C - 1)
-    flat_lane = iota((2 * C, width), 1)
+    deep = iota((spare, width), 0)
+    flat_lane = iota((spare, width), 1)
     wide_of = []
     for c in range(n_col):
         start = (deep - c * heads_here) * HEAD_DIM
         wide_of.append(((flat_lane >= start) & (flat_lane < start + HEAD_DIM)).astype(f32).astype(bf16))
-    for d in range(1, n_col):
-        den_copies[d - 1].wait_recv()
-        bottom = bottom + (den_recv[d - 1, :, :C].astype(f32) + den_recv[d - 1, :, C:].astype(f32))
-    inverse = jnp.where(iota((rows, C), 1) < heads, 1.0 / bottom, 0.0)
-    inverse_high = inverse.astype(bf16)
-    inverse = jnp.concatenate([inverse_high, (inverse - inverse_high.astype(f32)).astype(bf16)], axis=1)
-    factors = [query_gates[c, 1].astype(f32) * dot(inverse, wide_of[c]) for c in range(n_col)]
+    for copy in pushed[:1 - n_col]:
+        copy.wait_send()
     for copy in num_copies:
         copy.wait_recv()
+    for c in range(n_col):
+        for d in range(1, n_col):
+            arrived = num_recv[d - 1, c].astype(f32)
+            tops[c] = tops[c] + arrived[:, :width]
+            if c < 2:
+                bottom = bottom + arrived[:, width:]
+    inverse = jnp.where(iota((rows, spare), 1) < heads, 1.0 / bottom, 0.0)
+    inverse_high = inverse.astype(bf16)
+    inverse_low = (inverse - inverse_high.astype(f32)).astype(bf16)
     result = jnp.zeros((rows, width), f32)
     for c in range(n_col):
-        top = tops[c]
-        for d in range(1, n_col):
-            top = top + num_recv[d - 1, c].astype(f32)
-        result = result + dot((factors[c] * top).astype(bf16), aout_full[c])
+        factor = query_gates[c, 1].astype(f32) * (dot(inverse_high, wide_of[c]) + dot(inverse_low, wide_of[c]))
+        result = result + dot((factor * tops[c]).astype(bf16), aout_full[c])
     token_ref[...] = result.astype(bf16)
     store.wait()
-    for copy in pushed:
+    for copy in pushed[1 - n_col:]:
         copy.wait_send()
-
-
-def store_kernel(pair_src, token_src, pair_dst, token_dst, sems):
-    copies = [
-        pltpu.make_async_copy(pair_src, pair_dst, sems.at[0]),
-        pltpu.make_async_copy(token_src, token_dst, sems.at[1]),
-    ]
-    for copy in copies:
-        copy.start()
-    for copy in copies:
-        copy.wait()
 
 
 def on_device(n_row, n_col, pair_act, single, token_mask, chain_index, residue_index, tri_gain, tri_qk,
@@ -442,6 +429,7 @@
     width = attn_qk.shape[2]
     share = TRI_DIM // n_row
     per = cols // rows
+    lanes = -(-width // C) * C
     by_col = [pltpu.SemaphoreType.DMA((n_col - 1,))] * 2
     by_half = [pltpu.SemaphoreType.DMA((2, n_col - 1))] * 2
     by_row = [pltpu.SemaphoreType.DMA((n_row - 1,))] * 2
@@ -454,7 +442,7 @@
     )
     out_shape = (jax.ShapeDtypeStruct(pair_act.shape, bf16), jax.ShapeDtypeStruct((rows, width), bf16))
     everything = 64 * 1024 * 1024
-    results = pl.pallas_call(
+    return pl.pallas_call(
         functools.partial(kernel, n_row, n_col),
         out_shape=out_shape,
         in_specs=[pl.BlockSpec(memory_space=pltpu.HBM)] * 17,
@@ -472,25 +460,15 @@
             pltpu.VMEM((n_col, 8, C), f32),
             pltpu.VMEM((n_col, width, width), bf16),
             pltpu.VMEM((n_col, width, width), bf16),
-            pltpu.VMEM((n_col, rows, width), bf16),
-            pltpu.VMEM((n_col - 1, n_col, rows, width), bf16),
-            pltpu.VMEM((rows, 2 * C), bf16),
-            pltpu.VMEM((n_col - 1, rows, 2 * C), bf16),
+            pltpu.VMEM((n_col, rows, lanes), bf16),
+            pltpu.VMEM((n_col - 1, n_col, rows, lanes), bf16),
             pltpu.SemaphoreType.DMA((len(inputs),)),
             pltpu.SemaphoreType.DMA,
-        ] + by_half + by_row + by_row + by_row + by_col * 6,
+        ] + by_half + by_row + by_row + by_row + by_col * 5,
         compiler_params=pltpu.CompilerParams(
             collective_id=0, has_side_effects=True, vmem_limit_bytes=everything
         ),
     )(*inputs)
-    return pl.pallas_call(
-        store_kernel,
-        out_shape=out_shape,
-        in_specs=[pl.BlockSpec(memory_space=pltpu.HBM)] * 2,
-        out_specs=[pl.BlockSpec(memory_space=pltpu.HBM)] * 2,
-        scratch_shapes=[pltpu.SemaphoreType.DMA((2,))],
-        compiler_params=pltpu.CompilerParams(vmem_limit_bytes=everything),
-    )(*results)
 
 
 def solution(mesh):

time: 33.6 us -> 31.7 us (0.943)
  Pallas kernels: 32.8 us -> 28.7 us
  local copies, waits for them, and re-layouts: 0 us -> 2.18 us
    pallas_call x1 -> x0, Pallas kernels: 5.34 us -> none  [on_device(): pl.pallas_call(store_kernel, out_shape=out_shape, in_specs=[pl.BlockSpec(...]
    unnamed x0 -> x4, local copies, waits for them, and re-layouts: none -> 2.18 us
    pallas_call x1, Pallas kernels: 27.5 us -> 28.7 us  [on_device(): pl.pallas_call(functools.partial(kernel, n_row, n_col), out_shape=out_sha...]
where the time goes in v3:
time: 31.7 us; the launch traced here: 31.6 us
  Pallas kernels  28.7 us (91%)
  local copies, waits for them, and re-layouts  2.18 us (7%)
  between operations  0.65 us (2%)
    pallas_call x1, Pallas kernels, on_device(): pl.pallas_call(functools.partial(kernel, n_row, n_col), out_shape=out_sha...  28.7 us
    unnamed x4, local copies, waits for them, and re-layouts  2.18 us

profile of v3, /device:TPU:0, one launch (start us, length us, event | category | flops | bytes accessed | tf_op | source)
XLA Modules:
  0.0 31.6 jit_solution(17288457383366988636)
XLA Ops:
  0.6 28.7 %shard_map.176 = (bf16[16,32,128]{2,1,0:T(8,128)(2,1)}, bf16[16,192]{1,0:T(8,128)(2,1)}) custom-call(bf16[16,32,128]{2,1,0:T(8,128)(2,1)} %pair_hbm.1, bf16[16,768]{1,0:T(8,128)(2,1)} %single_hbm.1, s32[1,128]{1,0:T(1,128)} %bitcast.14, s32[1,128]{1,0:T(1,128)} %bitcast.15, s32[1,128]{1,0:T(1,128)} %bitcast.16, f32[2,128]{1,0:T(2,128)} %gain_hbm.1, ...), custom_call_target="tpu_custom_call" | custom-call | tf_op jit(solution)/shard_map/pallas_call | solution.py:445
  29.4 0.0 copy-start
  29.4 1.6 %copy.21 = bf16[16,32,128]{2,1,0:T(8,128)(2,1)} copy(bf16[16,32,128]{2,1,0:T(8,128)(2,1)} %get-tuple-element.4) | data formatting | bytes 262144
  31.0 0.0 copy-done
  31.0 0.6 %copy.22 = bf16[16,192]{1,0:T(8,128)(2,1)} copy(bf16[16,192]{1,0:T(8,128)(2,1)S(1)} %copy-done) | data formatting | bytes 12288
Async XLA Ops:
  29.4 1.6 %copy-start = (bf16[16,192]{1,0:T(8,128)(2,1)S(1)}, bf16[16,192]{1,0:T(8,128)(2,1)}, u32[]{:S(2)}) copy-start(bf16[16,192]{1,0:T(8,128)(2,1)} %get-tuple-element.5) | copy-start | bytes 18436

commit v4 on v3

--- a/solution.py
+++ b/solution.py
@@ -245,8 +245,6 @@
     for c in range(n_col):
         aout_send[c] = aout_ref[:, c * width:(c + 1) * width]
     aout_full[my_col] = aout_send[my_col]
-    aout_copies = push_cols(lambda d: aout_send.at[col_peers[d]], lambda d: aout_full.at[my_col],
-                            aout_send_sem, aout_recv_sem)
 
     loaded(out_ref, chain_ref, residue_ref, bias_gain_ref, bias_proj_ref)
     key_value_weight = jnp.concatenate([qk_ref[1, :, C:], vg_ref[1, :, :C]], axis=1)
@@ -317,6 +315,9 @@
     for d in far_first:
         ag_copies[d] = push(col_full.at[my_row], col_full.at[my_row], ag_send_sem.at[d - 1],
                             ag_recv_sem.at[d - 1], {"row": row_peers[d]})
+
+    aout_copies = push_cols(lambda d: aout_send.at[col_peers[d]], lambda d: aout_full.at[my_col],
+                            aout_send_sem, aout_recv_sem)
 
     head_shift = log2(heads)
     lines = rows * heads

time: 31.7 us -> 30.4 us (0.959)
  Pallas kernels: 28.7 us -> 27.5 us
    pallas_call x1, Pallas kernels: 28.7 us -> 27.5 us  [on_device(): pl.pallas_call(functools.partial(kernel, n_row, n_col), out_shape=out_sha...]
where the time goes in v4:
time: 30.4 us; the launch traced here: 30.3 us
  Pallas kernels  27.5 us (90%)
  local copies, waits for them, and re-layouts  2.18 us (7%)
  between operations  0.65 us (2%)
    pallas_call x1, Pallas kernels, on_device(): pl.pallas_call(functools.partial(kernel, n_row, n_col), out_shape=out_sha...  27.5 us
    unnamed x4, local copies, waits for them, and re-layouts  2.18 us

profile of v4, /device:TPU:0, one launch (start us, length us, event | category | flops | bytes accessed | tf_op | source)
XLA Modules:
  0.0 30.3 jit_solution(3051026245259807032)
XLA Ops:
  0.6 27.5 %shard_map.176 = (bf16[16,32,128]{2,1,0:T(8,128)(2,1)}, bf16[16,192]{1,0:T(8,128)(2,1)}) custom-call(bf16[16,32,128]{2,1,0:T(8,128)(2,1)} %pair_hbm.1, bf16[16,768]{1,0:T(8,128)(2,1)} %single_hbm.1, s32[1,128]{1,0:T(1,128)} %bitcast.14, s32[1,128]{1,0:T(1,128)} %bitcast.15, s32[1,128]{1,0:T(1,128)} %bitcast.16, f32[2,128]{1,0:T(2,128)} %gain_hbm.1, ...), custom_call_target="tpu_custom_call" | custom-call | tf_op jit(solution)/shard_map/pallas_call | solution.py:446
  28.1 0.0 copy-start
  28.1 1.6 %copy.21 = bf16[16,32,128]{2,1,0:T(8,128)(2,1)} copy(bf16[16,32,128]{2,1,0:T(8,128)(2,1)} %get-tuple-element.4) | data formatting | bytes 262144
  29.7 0.0 copy-done
  29.7 0.6 %copy.22 = bf16[16,192]{1,0:T(8,128)(2,1)} copy(bf16[16,192]{1,0:T(8,128)(2,1)S(1)} %copy-done) | data formatting | bytes 12288
Async XLA Ops:
  28.1 1.6 %copy-start = (bf16[16,192]{1,0:T(8,128)(2,1)S(1)}, bf16[16,192]{1,0:T(8,128)(2,1)}, u32[]{:S(2)}) copy-start(bf16[16,192]{1,0:T(8,128)(2,1)} %get-tuple-element.5) | copy-start | bytes 18436

commit v5 on v4

--- a/solution.py
+++ b/solution.py
@@ -228,10 +228,6 @@
     loaded(aqk_ref, avg_ref)
     kv[my_row, 0] = dot_nt(tok, aqk_ref[1]).astype(bf16)
     kv[my_row, 1] = dot_nt(tok, avg_ref[0]).astype(bf16)
-    kv_copies = {}
-    for d in far_first:
-        kv_copies[d] = push(kv.at[my_row], kv.at[my_row], kv_send_sem.at[d - 1],
-                            kv_recv_sem.at[d - 1], {"row": row_peers[d]})
     query_gate_weight = jnp.concatenate([qk_ref[0, :, :C], vg_ref[0, :, C:]], axis=1)
     feat_halves = []
     gate_halves = []
@@ -249,9 +245,14 @@
     loaded(out_ref, chain_ref, residue_ref, bias_gain_ref, bias_proj_ref)
     key_value_weight = jnp.concatenate([qk_ref[1, :, C:], vg_ref[1, :, :C]], axis=1)
     pairs, normed, key_feat, values = [], [], [], []
+    kv_copies = {}
     for b in range(2):
         for copy in row_copies[b]:
             copy.wait_recv()
+        if b == 0:
+            for d in far_first:
+                kv_copies[d] = push(kv.at[my_row], kv.at[my_row], kv_send_sem.at[d - 1],
+                                    kv_recv_sem.at[d - 1], {"row": row_peers[d]})
         lines = slice(b * half, (b + 1) * half)
         states = row_part[lines].astype(f32)
         for d in range(1, n_col):

time: 30.4 us -> 31.1 us (1.023)
  Pallas kernels: 27.5 us -> 28.1 us
    pallas_call x1, Pallas kernels: 27.5 us -> 28.1 us  [on_device(): pl.pallas_call(functools.partial(kernel, n_row, n_col), out_shape=out_sha...]
where the time goes in v5:
time: 31.1 us; the launch traced here: 31 us
  Pallas kernels  28.1 us (90%)
  local copies, waits for them, and re-layouts  2.18 us (7%)
  between operations  0.65 us (2%)
    pallas_call x1, Pallas kernels, on_device(): pl.pallas_call(functools.partial(kernel, n_row, n_col), out_shape=out_sha...  28.1 us
    unnamed x4, local copies, waits for them, and re-layouts  2.18 us

profile of v5, /device:TPU:0, one launch (start us, length us, event | category | flops | bytes accessed | tf_op | source)
XLA Modules:
  0.0 31.0 jit_solution(10570951502427291001)
XLA Ops:
  0.6 28.1 %shard_map.176 = (bf16[16,32,128]{2,1,0:T(8,128)(2,1)}, bf16[16,192]{1,0:T(8,128)(2,1)}) custom-call(bf16[16,32,128]{2,1,0:T(8,128)(2,1)} %pair_hbm.1, bf16[16,768]{1,0:T(8,128)(2,1)} %single_hbm.1, s32[1,128]{1,0:T(1,128)} %bitcast.14, s32[1,128]{1,0:T(1,128)} %bitcast.15, s32[1,128]{1,0:T(1,128)} %bitcast.16, f32[2,128]{1,0:T(2,128)} %gain_hbm.1, ...), custom_call_target="tpu_custom_call" | custom-call | tf_op jit(solution)/shard_map/pallas_call | solution.py:447
  28.8 0.0 copy-start
  28.8 1.6 %copy.21 = bf16[16,32,128]{2,1,0:T(8,128)(2,1)} copy(bf16[16,32,128]{2,1,0:T(8,128)(2,1)} %get-tuple-element.4) | data formatting | bytes 262144
  30.4 0.0 copy-done
  30.4 0.6 %copy.22 = bf16[16,192]{1,0:T(8,128)(2,1)} copy(bf16[16,192]{1,0:T(8,128)(2,1)S(1)} %copy-done) | data formatting | bytes 12288
Async XLA Ops:
  28.8 1.6 %copy-start = (bf16[16,192]{1,0:T(8,128)(2,1)S(1)}, bf16[16,192]{1,0:T(8,128)(2,1)}, u32[]{:S(2)}) copy-start(bf16[16,192]{1,0:T(8,128)(2,1)} %get-tuple-element.5) | copy-start | bytes 18436
